TPU v7x, 32 devices: a whole 2x2x4 slice. The times are simulated.
32 devices in a mesh: expert: 16 (over z, x, core), shard: 2 (over y).
Axes of the slice: x: 2, y: 2, z: 4, core: 2. Of those that a mesh axis runs over, the one named last changes fastest.
Arguments:
- tokens: bfloat16 [640, 4096], P('expert'), may hold values from -6 to 6
- expert_ids: int32 [640, 8], P('expert'), may hold values from 0 to 15, all different within a row; in each aligned block of 40 rows (0 to 39, 40 to 79, ...) at most 40 rows name the same one
- route_weights: float32 [640, 8], P('expert'), may hold values from 0.05 to 0.5
- partner: int32 [16], replicated, may hold values from 0 to 15, as said below
- gate_up: bfloat16 [16, 2, 768, 4096], P('expert', None, 'shard'), may hold values from -0.09375 to 0.09375
- down_weight: bfloat16 [16, 768, 4096], P('expert', None, 'shard'), may hold values from -0.21875 to 0.21875
- down_grad: bfloat16 [16, 128, 4096], P('expert', None, 'shard'), may hold values from -6 to 6
- moment_one: float32 [16, 128, 4096], P('expert', None, 'shard'), may hold values from -6 to 6
- moment_two: float32 [16, 128, 4096], P('expert', None, 'shard'), may hold values from 0.3 to 3
Outputs:
- combined: bfloat16 [640, 4096], P('expert', 'shard')
- trained_rows: bfloat16 [16, 128, 4096], P('expert', None, 'shard')
- first_moment: float32 [16, 128, 4096], P('expert', None, 'shard')
- second_moment: float32 [16, 128, 4096], P('expert', None, 'shard')
Inputs may be any that keep to these rules, and one draw needn't show every extreme that they name: `expert_ids`: each row names 8 different experts. In each aligned block of 40 rows (the rows held by one index of expert) no expert is named by more than 40 rows, a bound that some block reaches. partner[partner[p]] = p and partner[p] != p for every p: the list splits all 16 indices into pairs.
All inputs are finite; a program needn't handle non-finite values.
Results may differ from a plain program's by a relative error of at most 0.0058.
Values may be sent and summed in bfloat16 or wider, within the bound.
A program may use at most 64 MiB of HBM per device.

v0:
```python
import jax
import jax.numpy as jnp
from jax import lax
from jax.sharding import PartitionSpec as P

STEP = 100


learn_rate = 0.01
beta_one = 0.9
beta_two = 0.999
epsilon = 1e-08
decay_rate = 0.1


def adamw(weight, gradient, first, second):
    grad_wide = gradient.astype(jnp.float32)
    first_new = beta_one * first + (1.0 - beta_one) * grad_wide
    second_new = beta_two * second + (1.0 - beta_two) * grad_wide * grad_wide
    first_hat = first_new / (1.0 - beta_one**STEP)
    second_hat = second_new / (1.0 - beta_two**STEP)
    weight_wide = weight.astype(jnp.float32)
    updated = weight_wide - learn_rate * (
        first_hat / (jnp.sqrt(second_hat) + epsilon) + decay_rate * weight_wide
    )
    return (updated.astype(jnp.bfloat16), first_new, second_new)


def relocate(payload, partner):
    groups = lax.axis_size("expert")
    me = lax.axis_index("expert")

    def exchange(distance):
        pairs = [(i, i ^ distance) for i in range(groups)]
        return lambda block: lax.ppermute(block, "expert", pairs)

    offset = lax.bitwise_xor(me, partner[me])
    return lax.switch(offset - 1, [exchange(d) for d in range(1, groups)], payload)


def shards(
    tokens,
    expert_ids,
    route_weights,
    partner,
    gate_up,
    down_weight,
    down_grad,
    moment_one,
    moment_two,
):
    groups = lax.axis_size("expert")
    token_count = tokens.shape[0]
    model_width = tokens.shape[1]
    part_width = down_weight.shape[2]
    trained = down_grad.shape[1]
    capacity = 2 * token_count * expert_ids.shape[1] // groups
    new_rows, first_new, second_new = adamw(
        down_weight[:, :trained], down_grad, moment_one, moment_two
    )
    down_new = jnp.concatenate([new_rows, down_weight[:, trained:]], axis=1)
    wide = jnp.concatenate(
        [new_rows, first_new.astype(jnp.bfloat16), second_new.astype(jnp.bfloat16)], axis=0
    )
    arrived = relocate(wide, partner)
    rows_out = arrived[0:1]
    first_out = arrived[1:2].astype(jnp.float32)
    second_out = arrived[2:3].astype(jnp.float32)
    experts = jnp.arange(groups, dtype=jnp.int32)
    picked = (expert_ids[:, :, None] == experts[None, None, :]).astype(jnp.int32)
    running = jnp.cumsum(picked.reshape(-1, groups), axis=0).reshape(picked.shape)
    slot_index = jnp.sum((running - 1) * picked, axis=2)
    position = expert_ids * capacity + slot_index
    positions = jnp.arange(groups * capacity, dtype=jnp.int32)
    matches = position[None, :, :] == positions[:, None, None]
    dispatch = jnp.sum(matches.astype(jnp.int32), axis=2).astype(jnp.bfloat16)
    weighting = jnp.sum(jnp.where(matches, route_weights[None, :, :], 0.0), axis=2)
    outgoing = jnp.dot(dispatch, tokens, preferred_element_type=jnp.float32).astype(jnp.bfloat16)
    outgoing = outgoing.reshape(groups, capacity, tokens.shape[1])
    joined = gate_up.reshape(-1, model_width)
    hidden_count = joined.shape[0] // 2
    down_rows = down_new.reshape(-1, part_width)
    received = lax.all_to_all(outgoing, "expert", split_axis=0, concat_axis=0, tiled=True)
    leading = received.shape[:2]
    token_rows = received.reshape(-1, model_width)
    projected = lax.dot_general(
        token_rows, joined, (((1,), (1,)), ((), ())), preferred_element_type=jnp.float32
    )
    hidden = (jax.nn.silu(projected[:, :hidden_count]) * projected[:, hidden_count:]).astype(
        jnp.bfloat16
    )
    summed = jnp.dot(
        lax.all_gather(hidden, "shard", axis=1, tiled=True),
        down_rows,
        preferred_element_type=jnp.float32,
    )
    results = summed.astype(jnp.bfloat16).reshape(leading + (part_width,))
    returned = lax.all_to_all(results, "expert", split_axis=0, concat_axis=0, tiled=True)
    returned_wide = returned.reshape(-1, part_width).astype(jnp.float32)
    combined = jnp.dot(
        weighting.T,
        returned_wide,
        precision=lax.Precision.HIGHEST,
        preferred_element_type=jnp.float32,
    ).astype(jnp.bfloat16)
    return (combined, rows_out, first_out, second_out)


def solution(mesh):
    return jax.shard_map(
        shards,
        mesh=mesh,
        in_specs=(
            P("expert", None),
            P("expert", None),
            P("expert", None),
            P(),
            P("expert", None, "shard", None),
            P("expert", None, "shard"),
            P("expert", None, "shard"),
            P("expert", None, "shard"),
            P("expert", None, "shard"),
        ),
        out_specs=(
            P("expert", "shard"),
            P("expert", None, "shard"),
            P("expert", None, "shard"),
            P("expert", None, "shard"),
        ),
        check_vma=False,
    )
```

profile of v0, /device:TPU:1, one launch (start us, length us, event | category | flops | bytes accessed | tf_op | source)
XLA Modules:
  0.0 260.6 jit_solution(5430057876766765473)
XLA Ops:
  0.6 0.0 copy-start
  0.6 0.8 copy.20
  1.5 0.1 eq.37
  1.6 0.9 reduce-window.6
  2.4 0.2 slice_reduce_fusion
  2.7 0.1 bitcast_bitcast_fusion
  2.8 0.1 reduce_sum.30
  2.9 0.3 convert_reduce_fusion
  3.2 0.0 copy-done
  3.2 3.9 %convolution_convert_fusion = bf16[640,4096]{1,0:T(8,128)(2,1)} fusion(bf16[40,4096]{1,0:T(8,128)(2,1)S(1)} %copy-done, s32[640,40]{0,1:T(8,128)S(1)} %convert_reduce_fusion), kind=kOutput, calls=%fused_computation | convolution fusion | flops 212362240 | bytes 5672960 | tf_op jit(solution)/shard_map/dot_general | solution.py:78
  7.1 7.3 %all-to-all-start = ((bf16[16,40,4096]{2,1,0:T(8,128)(2,1)}), bf16[16,40,4096]{2,1,0:T(8,128)(2,1)}, u32[]{:S(2)}, u32[]{:S(2)}) async-start(bf16[16,40,4096]{2,1,0:T(8,128)(2,1)} %bitcast.28), calls=%async_computation | async-start | bytes 10485760 | tf_op jit(solution)/shard_map/all_to_all | solution.py:83
  14.5 0.0 copy-start.1
  14.5 0.0 copy-start.4
  14.5 0.0 copy-start.5
  14.5 1.9 copy-done.1
  16.4 0.3 copy-done.4
  16.6 0.3 copy-done.5
  17.0 3.4 %fusion.8 = (bf16[1,128,2048]{2,1,0:T(8,128)(2,1)}, bf16[1,128,2048]{2,1,0:T(8,128)(2,1)}, bf16[1,128,2048]{2,1,0:T(8,128)(2,1)}) fusion(bf16[1,128,2048]{2,1,0:T(8,128)(2,1)} %param.30, f32[1,128,2048]{2,1,0:T(8,128)S(1)} %copy-done.4, f32[1,128,2048]{2,1,0:T(8,128)S(1)} %copy-done.5, bf16[1,768,2048]{2,1,0:T(8,128)(2,1)S(1)} %copy-done.1), kind=kLoop, calls=%fused_computation.21 | loop fusion | flops 5242880 | bytes 4718592 | tf_op jit(solution)/shard_map/convert_element_type | solution.py:63
  20.4 90.5 %all-to-all-done = bf16[16,40,4096]{2,1,0:T(8,128)(2,1)} async-done(((bf16[16,40,4096]{2,1,0:T(8,128)(2,1)}), bf16[16,40,4096]{2,1,0:T(8,128)(2,1)}, u32[]{:S(2)}, u32[]{:S(2)}) %all-to-all-start) | async-done | bytes 5242912 | tf_op jit(solution)/shard_map/all_to_all | solution.py:83
  110.8 8.1 %fusion.14 = f32[640,768]{1,0:T(8,128)S(1)} fusion(bf16[640,4096]{1,0:T(8,128)(2,1)} %bitcast.2, bf16[768,4096]{1,0:T(8,128)(2,1)} %bitcast.32), kind=kOutput, calls=%fused_computation.38 | convolution fusion | flops 4026531840 | bytes 13500416 | tf_op jit(solution)/shard_map/dot_general | solution.py:86
  118.9 0.0 slice-start
  118.9 0.0 copy-start.3
  118.9 0.3 fusion.7
  119.2 13.9 %all_gather.3 = bf16[640,768]{1,0:T(8,128)(2,1)S(1)} all-gather(bf16[640,384]{1,0:T(8,128)(2,1)S(1)} %fusion.7), channel_id=1, replica_groups=mesh['expert'=16,'shard'=2] {'shard'}, dimensions={1}, use_global_device_ids=true | all-gather | bytes 1474560 | tf_op jit(solution)/shard_map/all_gather | solution.py:93
  133.1 0.0 slice-done
  133.1 0.0 copy-done.3
  133.1 3.7 %convolution_convert_fusion.1 = bf16[640,2048]{1,0:T(8,128)(2,1)} fusion(bf16[640,768]{1,0:T(8,128)(2,1)S(1)} %all_gather.3, bf16[1,640,2048]{2,1,0:T(8,128)(2,1)S(1)} %slice-done, bf16[1,128,2048]{2,1,0:T(8,128)(2,1)S(1)} %copy-done.3), kind=kOutput, calls=%fused_computation.1 | convolution fusion | flops 2020868096 | bytes 6750208 | tf_op jit(solution)/shard_map/dot_general | solution.py:92
  136.8 0.0 copy-start.6
  136.8 0.0 copy-start.7
  136.8 0.0 copy-start.2
  136.8 24.0 %all-to-all-start.1 = ((bf16[16,40,2048]{2,1,0:T(8,128)(2,1)}), bf16[16,40,2048]{2,1,0:T(8,128)(2,1)S(1)}, u32[]{:S(2)}, u32[]{:S(2)}) async-start(bf16[16,40,2048]{2,1,0:T(8,128)(2,1)} %bitcast.30), calls=%async_computation.1 | async-start | bytes 5242880 | tf_op jit(solution)/shard_map/all_to_all | solution.py:98
  160.8 0.0 copy-done.6
  160.8 0.1 copy.24
  160.9 0.0 copy-done.7
  160.9 0.6 dynamic_slice.3
  162.1 0.0 copy-done.2
  162.1 1.4 pad_maximum_fusion
  163.5 91.8 %conditional.1 = (bf16[3,128,2048]{2,1,0:T(8,128)(2,1)}) conditional(s32[]{:T(128)} %clamp.3, bf16[3,128,2048]{2,1,0:T(8,128)(2,1)S(1)} %pad_maximum_fusion, bf16[3,128,2048]{2,1,0:T(8,128)(2,1)S(1)} %pad_maximum_fusion, bf16[3,128,2048]{2,1,0:T(8,128)(2,1)S(1)} %pad_maximum_fusion, ...), branch_computations={%region_5.0_spmd, %region_6.0_spmd, %region_7.0_spmd, %region_8.0_... | conditional | bytes 6291504 | solution.py:38
  163.6 3.5 %collective-permute-start.10 = (bf16[3,128,2048]{2,1,0:T(8,128)(2,1)S(1)}, bf16[3,128,2048]{2,1,0:T(8,128)(2,1)}, u32[]{:S(2)}, u32[]{:S(2)}) collective-permute-start(bf16[3,128,2048]{2,1,0:T(8,128)(2,1)S(1)} %param.10), channel_id=1, source_target_pairs={{0,22},{2,20},{4,18},{6,16},{8,30},{10,28},{12,26},{14,24},{16,6},... | collective-permute-start | bytes 4718600 | tf_op jit(solution)/shard_map/cond/branch_10_fun/ppermute | solution.py:35
  167.0 88.2 %collective-permute-done.10 = bf16[3,128,2048]{2,1,0:T(8,128)(2,1)} collective-permute-done((bf16[3,128,2048]{2,1,0:T(8,128)(2,1)S(1)}, bf16[3,128,2048]{2,1,0:T(8,128)(2,1)}, u32[]{:S(2)}, u32[]{:S(2)}) %collective-permute-start.10) | collective-permute-done | bytes 1572896 | tf_op jit(solution)/shard_map/cond/branch_10_fun/ppermute | solution.py:35
  255.3 0.3 select_reduce_fusion
  255.6 3.0 %slice_convert_fusion = (f32[1,128,2048]{2,1,0:T(8,128)}, f32[1,128,2048]{2,1,0:T(8,128)}, bf16[1,128,2048]{2,1,0:T(8,128)(2,1)}) fusion(bf16[3,128,2048]{2,1,0:T(8,128)(2,1)} %get-tuple-element.41), kind=kLoop, calls=%fused_computation.23 | loop fusion | flops 524288 | bytes 4194304 | tf_op jit(solution)/shard_map/convert_element_type | solution.py:68
  258.6 0.0 all-to-all-done.1
  258.6 2.0 convolution_convert_fusion.2
  (5 shorter events, 0.1 us)
Async XLA Ops:
  0.6 2.6 copy-start
  7.1 103.7 %all-to-all-start = ((bf16[16,40,4096]{2,1,0:T(8,128)(2,1)}), bf16[16,40,4096]{2,1,0:T(8,128)(2,1)}, u32[]{:S(2)}, u32[]{:S(2)}) async-start(bf16[16,40,4096]{2,1,0:T(8,128)(2,1)} %bitcast.28), calls=%async_computation | async-start | bytes 10485760 | tf_op jit(solution)/shard_map/all_to_all | solution.py:83
  14.5 1.9 copy-start.1
  14.5 2.2 copy-start.4
  14.5 2.5 copy-start.5
  118.9 14.2 %slice-start = ((bf16[1,768,2048]{2,1,0:T(8,128)(2,1)}), bf16[1,640,2048]{2,1,0:T(8,128)(2,1)S(1)}, s32[]{:S(2)}) async-start(bf16[1,768,2048]{2,1,0:T(8,128)(2,1)} %param.29), calls=%async_computation.2 | async-start | bytes 5242880 | tf_op jit(solution)/shard_map/slice | solution.py:61
  118.9 14.2 %copy-start.3 = (bf16[1,128,2048]{2,1,0:T(8,128)(2,1)S(1)}, bf16[1,128,2048]{2,1,0:T(8,128)(2,1)}, u32[]{:S(2)}) copy-start(bf16[1,128,2048]{2,1,0:T(8,128)(2,1)} %get-tuple-element.39) | copy-start | bytes 1572868
  136.8 24.0 %copy-start.6 = (f32[40,8]{0,1:T(8,128)S(1)}, f32[40,8]{0,1:T(8,128)}, u32[]{:S(2)}) copy-start(f32[40,8]{0,1:T(8,128)} %param.26) | copy-start | bytes 3844
  136.8 24.1 %copy-start.7 = (s32[16]{0:T(128)S(1)}, s32[16]{0:T(128)}, u32[]{:S(2)}) copy-start(s32[16]{0:T(128)} %param.27) | copy-start | bytes 196
  136.8 25.3 %copy-start.2 = (bf16[1,128,2048]{2,1,0:T(8,128)(2,1)S(1)}, bf16[1,128,2048]{2,1,0:T(8,128)(2,1)}, u32[]{:S(2)}) copy-start(bf16[1,128,2048]{2,1,0:T(8,128)(2,1)} %get-tuple-element.38) | copy-start | bytes 1572868
  136.8 121.8 %all-to-all-start.1 = ((bf16[16,40,2048]{2,1,0:T(8,128)(2,1)}), bf16[16,40,2048]{2,1,0:T(8,128)(2,1)S(1)}, u32[]{:S(2)}, u32[]{:S(2)}) async-start(bf16[16,40,2048]{2,1,0:T(8,128)(2,1)} %bitcast.30), calls=%async_computation.1 | async-start | bytes 5242880 | tf_op jit(solution)/shard_map/all_to_all | solution.py:98
  163.6 91.7 %collective-permute-start.10 = (bf16[3,128,2048]{2,1,0:T(8,128)(2,1)S(1)}, bf16[3,128,2048]{2,1,0:T(8,128)(2,1)}, u32[]{:S(2)}, u32[]{:S(2)}) collective-permute-start(bf16[3,128,2048]{2,1,0:T(8,128)(2,1)S(1)} %param.10), channel_id=1, source_target_pairs={{0,22},{2,20},{4,18},{6,16},{8,30},{10,28},{12,26},{14,24},{16,6},... | collective-permute-start | bytes 4718600 | tf_op jit(solution)/shard_map/cond/branch_10_fun/ppermute | solution.py:35
where the time goes:
time: 261 us
  waiting for transfers between devices  179 us (69%)
  starting transfers between devices  34.8 us (13%)
  matrix products  17.7 us (7%)
  blocking collectives  13.9 us (5%)
  other arithmetic  9.68 us (4%)
  local copies, waits for them, and re-layouts  4.36 us (2%)
    all_to_all x1, waiting for transfers between devices, shards(): lax.all_to_all(outgoing, 'expert', split_axis=0, concat_axis=0, tiled=True)  90.5 us
    ppermute x1, waiting for transfers between devices, exchange(): return lambda block: lax.ppermute(block, 'expert', pairs)  88.2 us
    all_to_all x1, starting transfers between devices, shards(): lax.all_to_all(results, 'expert', split_axis=0, concat_axis=0, tiled=True)  24 us
    all_gather x1, blocking collectives, shards(): lax.all_gather(hidden, 'shard', axis=1, tiled=True)  13.9 us
    dot_general x1, matrix products, shards(): lax.dot_general(token_rows, joined, (((1,), (1,)), ((), ())), preferred_e...  8.08 us
    all_to_all x1, starting transfers between devices, shards(): lax.all_to_all(outgoing, 'expert', split_axis=0, concat_axis=0, tiled=True)  7.33 us
  transfers between devices with their start and end apart: 3, of which 2 were waited for; matrix products, arithmetic and copies ran while one was open for 3% of the time, Pallas kernels for 0%

commit v1 on v0

v1 whole, which is shorter than its diff:
```python
import functools

import jax
import jax.numpy as jnp
from jax import lax
from jax.experimental import pallas as pl
from jax.experimental.pallas import tpu as pltpu
from jax.sharding import PartitionSpec as P

STEP = 100


learn_rate = 0.01
beta_one = 0.9
beta_two = 0.999
epsilon = 1e-08
decay_rate = 0.1


def adamw(weight, gradient, first, second):
    grad_wide = gradient.astype(jnp.float32)
    first_new = beta_one * first + (1.0 - beta_one) * grad_wide
    second_new = beta_two * second + (1.0 - beta_two) * grad_wide * grad_wide
    first_hat = first_new / (1.0 - beta_one**STEP)
    second_hat = second_new / (1.0 - beta_two**STEP)
    weight_wide = weight.astype(jnp.float32)
    updated = weight_wide - learn_rate * (
        first_hat / (jnp.sqrt(second_hat) + epsilon) + decay_rate * weight_wide
    )
    return (updated.astype(jnp.bfloat16), first_new, second_new)


def relocate(payload, partner):
    groups = lax.axis_size("expert")
    me = lax.axis_index("expert")

    def exchange(distance):
        pairs = [(i, i ^ distance) for i in range(groups)]
        return lambda block: lax.ppermute(block, "expert", pairs)

    offset = lax.bitwise_xor(me, partner[me])
    return lax.switch(offset - 1, [exchange(d) for d in range(1, groups)], payload)


MESH_ID = pl.DeviceIdType.MESH
LANES = 128


def moe_kernel(A, B, S, rows, width, tok_ref, gate_ref, down_ref, new_ref, out_ref,
               slab, tok, gate, down, hid, part, got_core, acc, got_b, fin_in, got_a, tail_out, tail_in,
               local_sem, slab_s, slab_r, a_s, a_r, b_s, b_r, c_s, c_r, h_s, h_r,
               pc_s, pc_r, pb_s, pb_r, pa_s, pa_r, t_s, t_r):
    e = lax.axis_index("expert")
    y = lax.axis_index("shard")
    c = lax.rem(e, 2)
    chip = e // 2
    b = lax.rem(chip, B)
    a = chip // B
    half = tok.shape[2] // 2
    pair = 2 * rows
    units = hid.shape[3]
    cols = part.shape[2]
    hc = cols // 2
    trained = new_ref.shape[0]

    def expert_of(a1, b1, c1):
        return (a1 * B + b1) * 2 + c1

    def send(src, dst, ss, rs, target):
        copy = pltpu.make_async_remote_copy(
            src_ref=src, dst_ref=dst, send_sem=ss, recv_sem=rs,
            device_id=target, device_id_type=MESH_ID)
        copy.start()
        return copy

    def landed(dst, rs):
        pltpu.make_async_remote_copy(
            src_ref=dst, dst_ref=dst, send_sem=rs, recv_sem=rs,
            device_id=(expert_of(a, b, 1 - c), y), device_id_type=MESH_ID).wait_recv()

    loads = [
        pltpu.make_async_copy(gate_ref, gate, local_sem.at[0]),
        pltpu.make_async_copy(down_ref.at[pl.ds(trained, down.shape[0] - trained)],
                              down.at[pl.ds(trained, down.shape[0] - trained)], local_sem.at[1]),
        pltpu.make_async_copy(new_ref, down.at[pl.ds(0, trained)], local_sem.at[2]),
    ]
    for load in loads:
        load.start()

    core_dev = (expert_of(a, b, 1 - c), y)
    a_dev = [None] + [(expert_of(lax.rem(a + k, A), b, c), y) for k in range(1, A)]
    b_dev = [None] + [(expert_of(a, lax.rem(b + k, B), c), y) for k in range(1, B)]
    s_dev = [None] + [(e, lax.rem(y + k, S)) for k in range(1, S)]
    barrier = pltpu.get_barrier_semaphore()
    everyone = [core_dev] + a_dev[1:] + b_dev[1:] + s_dev[1:]
    for dev in everyone:
        pl.semaphore_signal(barrier, inc=1, device_id=dev, device_id_type=MESH_ID)
    pl.semaphore_wait(barrier, len(everyone))

    pending = [send(tok_ref, slab, slab_s, slab_r, core_dev)]
    landed(slab, slab_r)
    mine = tok_ref[...].astype(jnp.float32)
    other = slab[...].astype(jnp.float32)
    first = c == 0
    block = jnp.concatenate([jnp.where(first, mine, other), jnp.where(first, other, mine)], axis=0)

    def block_rows(k):
        return pl.ds(pl.multiple_of(lax.rem(a + k, A) * pair, 16), pair)

    my_cols = pl.ds(pl.multiple_of(c * half, LANES), half)
    peer_cols = pl.ds(pl.multiple_of((1 - c) * half, LANES), half)
    tok[b, block_rows(0), :] = block.astype(jnp.bfloat16)

    own = tok.at[b, block_rows(0), my_cols]
    for j in range(1, B):
        pending.append(send(own, own, b_s.at[j, 0], b_r.at[j, 0], b_dev[j]))
    for k in range(1, A):
        pending.append(send(own, own, a_s.at[k], a_r.at[k], a_dev[k]))
    for k in range(1, A):
        piece = tok.at[b, block_rows(A - k), my_cols]
        landed(piece, a_r.at[k])
        for j in range(1, B):
            pending.append(send(piece, piece, b_s.at[j, k], b_r.at[j, k], b_dev[j]))
        pending.append(send(piece, piece, c_s.at[0, k], c_r.at[0, k], core_dev))
    for k in range(1, A):
        landed(tok.at[b, block_rows(A - k), peer_cols], c_r.at[0, k])
    for load in loads:
        load.wait()

    def project(j):
        bj = lax.rem(b + B - j, B)
        x = tok[bj, :, :width]
        both = lax.dot_general(x, gate[...], (((1,), (1,)), ((), ())), preferred_element_type=jnp.float32)
        g = both[:, :units]
        hid[bj, y] = (g / (1.0 + jnp.exp(-g)) * both[:, units:]).astype(jnp.bfloat16)
        piece = hid.at[bj, y]
        for s in range(1, S):
            pending.append(send(piece, piece, h_s.at[j, s], h_r.at[j, s], s_dev[s]))

    def finish(j):
        bj = lax.rem(b + B - j, B)
        for s in range(1, S):
            landed(hid.at[bj, lax.rem(y + S - s, S)], h_r.at[j, s])
        total = jnp.dot(hid[bj, 0], down[pl.ds(0, units), :], preferred_element_type=jnp.float32)
        for s in range(1, S):
            total += jnp.dot(hid[bj, s], down[pl.ds(s * units, units), :], preferred_element_type=jnp.float32)
        lanes = lax.broadcasted_iota(jnp.int32, (A * pair, LANES), 1)
        high = tok[bj, :, width:width + LANES].astype(jnp.float32)
        low = tok[bj, :, width + LANES:width + 2 * LANES].astype(jnp.float32)
        weight = jnp.sum(jnp.where(lanes == e, high + low, 0.0), axis=1, keepdims=True)
        part[bj] = (total * weight).astype(jnp.bfloat16)
        pending.append(send(part.at[bj, :, pl.ds(pl.multiple_of((1 - c) * hc, LANES), hc)],
                            got_core.at[bj], pc_s.at[j], pc_r.at[j], core_dev))

    def join(j):
        bj = lax.rem(b + B - j, B)
        landed(got_core.at[bj], pc_r.at[j])
        acc[j] = (part[bj, :, pl.ds(pl.multiple_of(c * hc, LANES), hc)].astype(jnp.float32)
                  + got_core[bj].astype(jnp.float32)).astype(jnp.bfloat16)
        if j:
            for k in range(A):
                src = acc.at[j, block_rows((k + 1) % A)]
                dst = got_b.at[j, block_rows((k + 1) % A)]
                pending.append(send(src, dst, pb_s.at[j, k], pb_r.at[j, k], b_dev[B - j]))

    project(0)
    for j in range(1, B):
        for k in range(A):
            landed_rows = block_rows(A - k)
            piece = tok.at[lax.rem(b + B - j, B), landed_rows, my_cols]
            landed(piece, b_r.at[j, k])
            pending.append(send(piece, piece, c_s.at[j, k], c_r.at[j, k], core_dev))
        if j == 1:
            finish(0)
        for k in range(A):
            landed(tok.at[lax.rem(b + B - j, B), block_rows(A - k), peer_cols], c_r.at[j, k])
        project(j)
        if j == 1:
            join(0)
        finish(j)
        join(j)
    final = None
    for k in range(A):
        where = block_rows((k + 1) % A)
        total = acc[0, where, :].astype(jnp.float32)
        for j in range(1, B):
            landed(got_b.at[j, where], pb_r.at[j, k])
            total += got_b[j, where, :].astype(jnp.float32)
        if k < A - 1:
            fin_in[k + 1] = total.astype(jnp.bfloat16)
            pending.append(send(fin_in.at[k + 1], got_a.at[k + 1], pa_s.at[k + 1], pa_r.at[k + 1], a_dev[k + 1]))
        else:
            final = total
    for k in range(1, A):
        landed(got_a.at[k], pa_r.at[k])
        final += got_a[k].astype(jnp.float32)
    low_rows, high_rows = final[:rows], final[rows:]
    tail_out[...] = jnp.where(first, high_rows, low_rows).astype(jnp.bfloat16)
    pending.append(send(tail_out, tail_in, t_s, t_r, core_dev))
    out_ref[:, pl.ds(pl.multiple_of(c * hc, LANES), hc)] = jnp.where(first, low_rows, high_rows).astype(jnp.bfloat16)
    landed(tail_in, t_r)
    out_ref[:, pl.ds(pl.multiple_of((1 - c) * hc, LANES), hc)] = tail_in[...]
    for copy in pending:
        copy.wait_send()


def experts_layer(tokens, weighting, gate_up, down_weight, new_rows):
    groups = lax.axis_size("expert")
    S = lax.axis_size("shard")
    rows, width = tokens.shape
    B = groups // 8
    A = 4
    hidden_units, cols = down_weight.shape
    units = hidden_units // S
    fill = ((0, 0), (0, LANES - groups))
    high = lax.reduce_precision(weighting, 8, 7)
    low = weighting - high
    extended = jnp.concatenate(
        [tokens, jnp.pad(high, fill).astype(jnp.bfloat16), jnp.pad(low, fill).astype(jnp.bfloat16)], axis=1)
    wide = width + 2 * LANES
    bf = jnp.bfloat16
    hc = cols // 2
    group_rows = 2 * A * rows
    dma = pltpu.SemaphoreType.DMA
    scratch = [
        pltpu.VMEM((rows, wide), bf),
        pltpu.VMEM((B, group_rows, wide), bf),
        pltpu.VMEM((2 * units, width), bf),
        pltpu.VMEM((hidden_units, cols), bf),
        pltpu.VMEM((B, S, group_rows, units), bf),
        pltpu.VMEM((B, group_rows, cols), bf),
        pltpu.VMEM((B, group_rows, hc), bf),
        pltpu.VMEM((B, group_rows, hc), bf),
        pltpu.VMEM((B, group_rows, hc), bf),
        pltpu.VMEM((A, 2 * rows, hc), bf),
        pltpu.VMEM((A, 2 * rows, hc), bf),
        pltpu.VMEM((rows, hc), bf),
        pltpu.VMEM((rows, hc), bf),
        dma((3,)), dma, dma, dma((A,)), dma((A,)), dma((B, A)), dma((B, A)), dma((B, A)), dma((B, A)),
        dma((B, S)), dma((B, S)), dma((B,)), dma((B,)), dma((B, A)), dma((B, A)), dma((A,)), dma((A,)), dma, dma,
    ]
    return pl.pallas_call(
        functools.partial(moe_kernel, A, B, S, rows, width),
        out_shape=jax.ShapeDtypeStruct((rows, cols), bf),
        in_specs=[pl.BlockSpec(memory_space=pltpu.VMEM)] + [pl.BlockSpec(memory_space=pl.ANY)] * 3,
        out_specs=pl.BlockSpec(memory_space=pltpu.VMEM),
        scratch_shapes=scratch,
        compiler_params=pltpu.CompilerParams(
            collective_id=0, has_side_effects=True, vmem_limit_bytes=60 * 1024 * 1024),
    )(extended, gate_up, down_weight, new_rows)


def shards(
    tokens,
    expert_ids,
    route_weights,
    partner,
    gate_up,
    down_weight,
    down_grad,
    moment_one,
    moment_two,
):
    groups = lax.axis_size("expert")
    trained = down_grad.shape[1]
    new_rows, first_new, second_new = adamw(
        down_weight[:, :trained], down_grad, moment_one, moment_two
    )
    experts = jnp.arange(groups, dtype=jnp.int32)
    picked = expert_ids[:, :, None] == experts[None, None, :]
    weighting = jnp.sum(jnp.where(picked, route_weights[:, :, None], 0.0), axis=1)
    combined = experts_layer(
        tokens, weighting, gate_up.reshape(-1, gate_up.shape[3]), down_weight[0], new_rows[0]
    )
    wide = jnp.concatenate(
        [new_rows, first_new.astype(jnp.bfloat16), second_new.astype(jnp.bfloat16)], axis=0
    )
    arrived = relocate(wide, partner)
    rows_out = arrived[0:1]
    first_out = arrived[1:2].astype(jnp.float32)
    second_out = arrived[2:3].astype(jnp.float32)
    return (combined, rows_out, first_out, second_out)


def solution(mesh):
    return jax.shard_map(
        shards,
        mesh=mesh,
        in_specs=(
            P("expert", None),
            P("expert", None),
            P("expert", None),
            P(),
            P("expert", None, "shard", None),
            P("expert", None, "shard"),
            P("expert", None, "shard"),
            P("expert", None, "shard"),
            P("expert", None, "shard"),
        ),
        out_specs=(
            P("expert", "shard"),
            P("expert", None, "shard"),
            P("expert", None, "shard"),
            P("expert", None, "shard"),
        ),
        check_vma=False,
    )
```

time: 261 us -> 140 us (0.54)
  waiting for transfers between devices: 179 us -> 35.1 us
  Pallas kernels: 0 us -> 89.4 us
  starting transfers between devices: 34.8 us -> 0.07 us
  matrix products: 17.7 us -> 0 us
  blocking collectives: 13.9 us -> 0 us
    all_to_all x2 -> x0, waiting for transfers between devices: 90.5 us -> none  [the longest x1 90.5 us: shards(): lax.all_to_all(outgoing, 'expert', split_axis=0, concat_axis=0, tiled=True)]
    pallas_call x0 -> x1, Pallas kernels: none -> 89.4 us  [experts_layer(): pl.pallas_call(functools.partial(moe_kernel, A, B, S, rows, width), out_s...]
    ppermute x1, waiting for transfers between devices: 88.2 us -> 35.1 us  [exchange(): return lambda block: lax.ppermute(block, 'expert', pairs)]
    all_to_all x2 -> x0, starting transfers between devices: 31.3 us -> none  [the longest x1 24 us: shards(): lax.all_to_all(results, 'expert', split_axis=0, concat_axis=0, tiled=True)]
    dot_general x4 -> x0, matrix products: 17.7 us -> none  [the longest x1 8.08 us: shards(): lax.dot_general(token_rows, joined, (((1,), (1,)), ((), ())), preferred_e...]
    all_gather x1 -> x0, blocking collectives: 13.9 us -> none  [shards(): lax.all_gather(hidden, 'shard', axis=1, tiled=True)]
    ppermute x1, starting transfers between devices: 3.5 us -> 0.07 us  [exchange(): return lambda block: lax.ppermute(block, 'expert', pairs)]
    unnamed x18 -> x5, local copies, waits for them, and re-layouts: 3.38 us -> 0.67 us
  transfers between devices with their start and end apart: 3 -> 1, of which waited for: 2 -> 1; matrix products, arithmetic and copies ran while one was open for 3% -> 0% of each run, Pallas kernels for 0% -> 0%
where the time goes in v1:
time: 140 us; the launch traced here: 137 us
  Pallas kernels  89.4 us (64%)
  waiting for transfers between devices  35.1 us (25%)
  other arithmetic  9.2 us (7%)
  local copies, waits for them, and re-layouts  2.07 us (1%)
    pallas_call x1, Pallas kernels, experts_layer(): pl.pallas_call(functools.partial(moe_kernel, A, B, S, rows, width), out_s...  89.4 us
    ppermute x1, waiting for transfers between devices, exchange(): return lambda block: lax.ppermute(block, 'expert', pairs)  35.1 us
    convert_element_type x1, other arithmetic, shards(): first_new.astype(jnp.bfloat16)  3.57 us
    convert_element_type x1, other arithmetic, shards(): second_out = arrived[2:3].astype(jnp.float32)  2.99 us
  transfers between devices with their start and end apart: 1, of which 1 were waited for; matrix products, arithmetic and copies ran while one was open for 0% of the time, Pallas kernels for 0%

profile of v1, /device:TPU:1, one launch (start us, length us, event | category | flops | bytes accessed | tf_op | source)
XLA Modules:
  0.0 137.2 jit_solution(18051098229047594387)
XLA Ops:
  0.6 1.2 dynamic_slice.3
  2.5 0.7 select_reduce_fusion
  3.3 0.1 copy.18
  3.3 0.1 copy.17
  3.4 1.7 %fusion.11.tok_ref = bf16[40,4352]{1,0:T(8,128)(2,1)} fusion(bf16[40,16]{1,0:T(8,128)(2,1)S(1)} %get-tuple-element.42, bf16[40,16]{1,0:T(8,128)(2,1)S(1)} %get-tuple-element.41, bf16[40,4096]{1,0:T(8,128)(2,1)} %param.24), kind=kLoop, calls=%fused_computation.21 | loop fusion | flops 2088960 | bytes 678400 | tf_op jit(solution)/shard_map/concatenate | solution.py:218
  5.2 3.6 %fusion.8 = (bf16[1,128,2048]{2,1,0:T(8,128)(2,1)S(1)}, bf16[1,128,2048]{2,1,0:T(8,128)(2,1)}, bf16[1,128,2048]{2,1,0:T(8,128)(2,1)S(1)}) fusion(bf16[1,128,2048]{2,1,0:T(8,128)(2,1)} %param.30, f32[1,128,2048]{2,1,0:T(8,128)} %param.31, f32[1,128,2048]{2,1,0:T(8,128)} %param.32, bf16[1,768,2048]{2,1,0:T(8,128)(2,1)} %param.29), kind=kLoop, calls=%fused_computation.16 | loop fusion | flops 5242880 | bytes 4718592 | tf_op jit(solution)/shard_map/convert_element_type | solution.py:276
  8.7 0.0 copy-start
  8.7 89.4 %shard_map.120 = bf16[40,2048]{1,0:T(8,128)(2,1)} custom-call(bf16[40,4352]{1,0:T(8,128)(2,1)} %fusion.11.tok_ref, bf16[768,4096]{1,0:T(8,128)(2,1)} %bitcast.4, bf16[768,2048]{1,0:T(8,128)(2,1)} %bitcast.6, bf16[128,2048]{1,0:T(8,128)(2,1)} %bitcast.5), custom_call_target="tpu_custom_call" | custom-call | tf_op jit(solution)/shard_map/pallas_call | solution.py:242
  98.1 0.0 copy-done
  98.1 0.2 pad_maximum_fusion
  98.3 35.2 %conditional.1 = (bf16[3,128,2048]{2,1,0:T(8,128)(2,1)}) conditional(s32[]{:T(128)} %clamp.3, bf16[3,128,2048]{2,1,0:T(8,128)(2,1)S(1)} %pad_maximum_fusion, bf16[3,128,2048]{2,1,0:T(8,128)(2,1)S(1)} %pad_maximum_fusion, bf16[3,128,2048]{2,1,0:T(8,128)(2,1)S(1)} %pad_maximum_fusion, ...), branch_computations={%region_1.2_spmd, %region_2.3_spmd, %region_3.4_spmd, %region_4.5_... | conditional | bytes 6291504 | solution.py:42
  98.4 0.1 collective-permute-start.3
  98.4 35.1 %collective-permute-done.3 = bf16[3,128,2048]{2,1,0:T(8,128)(2,1)} collective-permute-done((bf16[3,128,2048]{2,1,0:T(8,128)(2,1)S(1)}, bf16[3,128,2048]{2,1,0:T(8,128)(2,1)}, u32[]{:S(2)}, u32[]{:S(2)}) %collective-permute-start.3) | collective-permute-done | bytes 1572896 | tf_op jit(solution)/shard_map/cond/branch_3_fun/ppermute | solution.py:39
  133.5 0.0 copy-start.1
  133.5 3.0 %slice_convert_fusion = (f32[1,128,2048]{2,1,0:T(8,128)}, f32[1,128,2048]{2,1,0:T(8,128)}, bf16[1,128,2048]{2,1,0:T(8,128)(2,1)}) fusion(bf16[3,128,2048]{2,1,0:T(8,128)(2,1)} %get-tuple-element.51), kind=kLoop, calls=%fused_computation.18 | loop fusion | flops 524288 | bytes 4194304 | tf_op jit(solution)/shard_map/convert_element_type | solution.py:281
  136.5 0.0 copy-done.1
  136.5 0.7 copy.36
  (2 shorter events, 0.0 us)
Async XLA Ops:
  8.7 89.4 %copy-start = (bf16[1,128,2048]{2,1,0:T(8,128)(2,1)S(1)}, bf16[1,128,2048]{2,1,0:T(8,128)(2,1)}, u32[]{:S(2)}) copy-start(bf16[1,128,2048]{2,1,0:T(8,128)(2,1)} %get-tuple-element.39) | copy-start | bytes 1572868
  98.4 35.2 %collective-permute-start.3 = (bf16[3,128,2048]{2,1,0:T(8,128)(2,1)S(1)}, bf16[3,128,2048]{2,1,0:T(8,128)(2,1)}, u32[]{:S(2)}, u32[]{:S(2)}) collective-permute-start(bf16[3,128,2048]{2,1,0:T(8,128)(2,1)S(1)} %param.3), channel_id=1, source_target_pairs={{0,8},{2,10},{4,12},{6,14},{8,0},{10,2},{12,4},{14,6},{16,24},{18,... | collective-permute-start | bytes 4718600 | tf_op jit(solution)/shard_map/cond/branch_3_fun/ppermute | solution.py:39
  133.5 3.0 %copy-start.1 = (bf16[40,2048]{1,0:T(8,128)(2,1)S(1)}, bf16[40,2048]{1,0:T(8,128)(2,1)}, u32[]{:S(2)}) copy-start(bf16[40,2048]{1,0:T(8,128)(2,1)} %shard_map.120) | copy-start | bytes 491524
